TPU v7x, 512 devices: a whole 4x4x16 slice. The times are simulated.
512 devices in a mesh: seq: 64 (over z, y), vocab: 8 (over x, core).
Axes of the slice: x: 4, y: 4, z: 16, core: 2. Of those that a mesh axis runs over, the one named last changes fastest.
Arguments:
- queries: bfloat16 [512, 8192], P('seq'), may hold values from -32 to 32
- cached_keys: bfloat16 [32768, 1024], P(('seq', 'vocab')), may hold values from -12 to 12
- cached_values: bfloat16 [32768, 1024], P(('seq', 'vocab')), may hold values from -6 to 6
- out_weight: bfloat16 [8192, 5120], P('seq', 'vocab'), may hold values from -0.25 to 0.25
- residual: bfloat16 [512, 5120], P('seq', 'vocab'), may hold values from -64 to 64
- norm_gain: bfloat16 [5120], replicated, may hold values from 0.5 to 1.5
- head_weight: bfloat16 [151552, 5120], P(('seq', 'vocab')), may hold values from -1 to 1
- targets: int32 [512], replicated, may hold values from 0 to 151551
- span_offset: int32 [1], replicated, may hold values from 0 to 32256
Outputs:
- logprob: float32 [512], P('seq')
All inputs are finite; a program needn't handle non-finite values.
Results may differ from a plain program's by a relative error of at most 0.0085.
Values may be sent and summed in bfloat16 or wider, within the bound.
A program may use at most 64 MiB of HBM per device.

v0:
```python
import math

import jax
import jax.numpy as jnp
from jax import lax
from jax.experimental import pallas as pl
from jax.experimental.pallas import tpu as pltpu
from jax.sharding import PartitionSpec as P

MESH = pl.DeviceIdType.MESH
HEAD_DIM = 128
NZ, NY, NX, NC = 16, 4, 4, 2
NV = NX * NC
WIDTH = 5120
COLS = WIDTH // NV
ROWS = 296
FLOOR = 1e-06
LOW = -1e30
F32 = jnp.float32
BF16 = jnp.bfloat16


def split3(x):
    hi = x.astype(BF16).astype(F32)
    rest = x - hi
    mid = rest.astype(BF16).astype(F32)
    lo = (rest - mid).astype(BF16).astype(F32)
    return hi, mid, lo


def nt(a, b, precision=None):
    return lax.dot_general(
        a, b, (((1,), (1,)), ((), ())), preferred_element_type=F32, precision=precision
    )


def kernel(
    span_ref,
    q_ref,
    k_ref,
    v_ref,
    w_ref,
    res_ref,
    gain_ref,
    ginv_ref,
    head_ref,
    tgt_ref,
    out_ref,
    q1src,
    q1buf,
    qall,
    kvbuf,
    vt,
    sbuf,
    osend,
    obuf,
    psrc,
    pbuf,
    att,
    abuf,
    wbuf,
    prsend,
    prbuf,
    hsend,
    hall,
    whead,
    logit,
    stsrc,
    stbuf,
    stplane,
    stz,
    kv_s,
    kv_r,
    q1_s,
    q1_r,
    kf_s,
    kf_r,
    qa_s,
    qa_r,
    o_s,
    o_r,
    p_s,
    p_r,
    a_s,
    a_r,
    w_s,
    w_r,
    pr_s,
    pr_r,
    h_s,
    h_r,
    h1_s,
    h1_r,
    h2_s,
    h2_r,
    hw_s,
    hw_r,
    t1_s,
    t1_r,
    t2_s,
    t2_r,
    loc,
):
    s = lax.axis_index("seq")
    v = lax.axis_index("vocab")
    z, y, x, c = s // NY, s % NY, v // NC, v % NC
    g, par = z // 2, z % 2

    def dev(zz, yy, xx, cc):
        return (zz * NY + yy, xx * NC + cc)

    def wrap(a, n):
        return lax.rem(a + n, n)

    def push(src, dst, ss, rs, to):
        cp = pltpu.make_async_remote_copy(
            src_ref=src, dst_ref=dst, send_sem=ss, recv_sem=rs, device_id=to, device_id_type=MESH
        )
        cp.start()

    def got(ref, sem):
        pltpu.make_async_copy(ref, ref, sem).wait()

    own_head = pltpu.make_async_copy(head_ref, whead.at[0], loc.at[0])
    own_head.start()
    own_w = pltpu.make_async_copy(w_ref, wbuf.at[y], loc.at[1])
    own_w.start()
    own_k = pltpu.make_async_copy(
        k_ref.at[:, pl.ds(pl.multiple_of(g * 128, 128), 128)], kvbuf.at[y, g, 0], loc.at[2]
    )
    own_k.start()
    own_v = pltpu.make_async_copy(
        v_ref.at[:, pl.ds(pl.multiple_of(g * 128, 128), 128)], kvbuf.at[y, g, 1], loc.at[3]
    )
    own_v.start()

    barrier = pltpu.get_barrier_semaphore()

    def greet(zz, yy, xx, cc):
        pl.semaphore_signal(barrier, inc=1, device_id=dev(zz, yy, xx, cc), device_id_type=MESH)

    @pl.loop(1, NZ)
    def _(d):
        greet(wrap(z + d, NZ), y, x, c)
        greet(wrap(z + d, NZ), y, x, 1 - c)

    greet(z, y, x, 1 - c)
    for dx in range(1, NX):
        greet(z, y, wrap(x + dx, NX), 1 - c)
    for dy in range(NY):
        for dx in range(NX):
            if (dy, dx) != (0, 0):
                greet(z, wrap(y + dy, NY), wrap(x + dx, NX), c)

    q_f = q_ref[...].astype(F32)
    pick_row = lax.broadcasted_iota(jnp.int32, (8, 128), 0) == v
    for h in range(64):
        row = jnp.sum(
            jnp.where(pick_row, q_f[:, h * 128 : (h + 1) * 128], 0.0), axis=0, keepdims=True
        )
        q1src[h // 8, h % 8 : h % 8 + 1, :] = row

    pl.semaphore_wait(barrier, 2 * (NZ - 1) + 1 + (NX - 1) + NY * NX - 1)

    @pl.loop(1, NZ)
    def _(d):
        to = wrap(z + d, NZ)
        push(q1src.at[to // 2], q1buf.at[z], q1_s.at[d], q1_r.at[z], dev(to, y, x, c))

    @pl.loop(1, 8)
    def _(d):
        head = wrap(g + d, 8)
        to = dev(2 * head + par, y, x, c)
        cols = pl.ds(pl.multiple_of(head * 128, 128), 128)
        push(k_ref.at[:, cols], kvbuf.at[y, g, 0], kv_s.at[d, 0], kv_r.at[g, 0], to)
        push(v_ref.at[:, cols], kvbuf.at[y, g, 1], kv_s.at[d, 1], kv_r.at[g, 1], to)

    for d in range(1, NY):
        push(w_ref, wbuf.at[y], w_s.at[d], w_r.at[y], dev(z, wrap(y + d, NY), x, c))
    push(head_ref, whead.at[1], hw_s.at[0], hw_r.at[0], dev(z, y, x, 1 - c))

    q1buf[z] = q1src[g]

    @pl.loop(1, NZ)
    def _(d):
        frm = wrap(z - d + NZ, NZ)
        got(q1buf.at[frm], q1_r.at[frm])

    ri = lax.broadcasted_iota(jnp.int32, (128, 128), 0)
    ci = lax.broadcasted_iota(jnp.int32, (128, 128), 1)
    to_heads = (ci == (ri % 16) * 8 + ri // 16).astype(BF16)
    q_rows = q1buf[...].reshape(128, 128).astype(BF16)
    qall[v] = jnp.dot(to_heads, q_rows, preferred_element_type=F32).astype(BF16)

    @pl.loop(1, NV)
    def _(k):
        o = wrap(v + k, NV)
        push(qall.at[v], qall.at[v], qa_s.at[k], qa_r.at[v], dev(z, y, o // NC, o % NC))

    own_k.wait()
    own_v.wait()

    @pl.loop(0, 8)
    def _(d):
        frm = wrap(g - d + 8, 8)

        @pl.when(d > 0)
        def _():
            got(kvbuf.at[y, frm, 0], kv_r.at[frm, 0])
            got(kvbuf.at[y, frm, 1], kv_r.at[frm, 1])

        for e in range(1, NY):
            push(
                kvbuf.at[y, frm],
                kvbuf.at[y, frm],
                kf_s.at[frm, e],
                kf_r.at[y, frm],
                dev(z, wrap(y + e, NY), x, c),
            )

    for e in range(1, NY):
        frm_y = wrap(y - e + NY, NY)

        @pl.loop(0, 8)
        def _(j):
            got(kvbuf.at[frm_y, j], kf_r.at[frm_y, j])

    for yy in range(NY):
        vt[:, yy * 512 : (yy + 1) * 512] = kvbuf[yy, :, 1].reshape(512, 128).T

    span = span_ref[0]
    scale = 1.0 / math.sqrt(HEAD_DIM)
    rho = lax.broadcasted_iota(jnp.int32, (512, 128), 0)
    lane = lax.broadcasted_iota(jnp.int32, (512, 128), 1)
    pos = (rho // 64) * 4096 + rho % 64 + ((4 * par) * 8 + v) * 64
    tok = 8 * (4 * (lane % 16) + y) + span

    @pl.loop(1, NV + 1)
    def _(k):
        o = wrap(v + k, NV)

        @pl.when(k < NV)
        def _():
            got(qall.at[o], qa_r.at[o])

        q_blk = qall[o]
        top = jnp.full((1, 128), LOW, F32)
        for yy in range(NY):
            scores = nt(kvbuf[yy, :, 0].reshape(512, 128), q_blk) * scale
            live = pos + yy * 512 <= tok + o
            scores = jnp.where(live, scores, LOW)
            sbuf[yy] = scores
            top = jnp.maximum(top, jnp.max(scores, axis=0, keepdims=True))
        total = jnp.zeros((1, 128), F32)
        acc = jnp.zeros((128, 128), F32)
        for yy in range(NY):
            live = pos + yy * 512 <= tok + o
            wts = jnp.where(live, jnp.exp(sbuf[yy] - top), 0.0)
            total = total + jnp.sum(wts, axis=0, keepdims=True)
            acc = acc + jnp.dot(
                vt[:, yy * 512 : (yy + 1) * 512], wts.astype(BF16), preferred_element_type=F32
            )
        stats = jnp.concatenate(
            list(split3(top)) + list(split3(total)) + [jnp.zeros((10, 128), F32)], axis=0
        )
        osend[o, 0:128, :] = acc.astype(BF16)
        osend[o, 128:144, :] = stats.astype(BF16)

        @pl.when(k < NV)
        def _():
            push(osend.at[o], obuf.at[v], o_s.at[k], o_r.at[v], dev(z, y, o // NC, o % NC))

    def unpack(block):
        b = block.astype(F32)
        return (
            b[128:129] + b[129:130] + b[130:131],
            b[131:132] + b[132:133] + b[133:134],
            b[0:128],
        )

    def blend(one, two):
        m1, l1, a1 = one
        m2, l2, a2 = two
        m = jnp.maximum(m1, m2)
        f1, f2 = jnp.exp(m1 - m), jnp.exp(m2 - m)
        return m, l1 * f1 + l2 * f2, a1 * f1 + a2 * f2

    def take_share(k, state):
        frm = wrap(v - k + NV, NV)
        got(obuf.at[frm], o_r.at[frm])
        return blend(state, unpack(obuf[frm]))

    state = lax.fori_loop(1, NV, take_share, unpack(osend[v]))

    m_own, l_own, a_own = state
    stats = jnp.concatenate(
        list(split3(m_own)) + list(split3(l_own)) + [jnp.zeros((10, 128), F32)], axis=0
    )
    psrc[0:128, :] = a_own.astype(BF16)
    psrc[128:144, :] = stats.astype(BF16)
    push(psrc, pbuf, p_s.at[0], p_r.at[0], dev(z + 1 - 2 * par, y, x, c))
    got(pbuf, p_r.at[0])
    _, l_all, a_all = blend(state, unpack(pbuf[...]))
    att[...] = (a_all / l_all).T.astype(BF16)

    mine = att.at[pl.ds(pl.multiple_of(par * 64, 64), 64)]

    @pl.loop(1, NV)
    def _(k):
        o = wrap(v + k, NV)
        push(mine, abuf.at[v], a_s.at[k], a_r.at[v], dev(z, y, o // NC, o % NC))

    abuf[v] = att[pl.ds(pl.multiple_of(par * 64, 64), 64), :]
    own_w.wait()
    for d in range(1, NY):
        frm_y = wrap(y - d + NY, NY)
        got(wbuf.at[frm_y], w_r.at[frm_y])

    @pl.loop(1, NV)
    def _(k):
        frm = wrap(v - k + NV, NV)
        got(abuf.at[frm], a_r.at[frm])

    proj = jnp.zeros((128, COLS), F32)
    for h in range(4):
        rows = abuf[:, h * 16 : (h + 1) * 16, :].reshape(128, 128)
        proj = proj + jnp.dot(rows, wbuf[h], preferred_element_type=F32)
    to_planes = (ci == (ri % 8) * 16 + ri // 8).astype(BF16)
    by_plane = jnp.dot(to_planes, proj.astype(BF16), preferred_element_type=F32)
    prsend[...] = by_plane.reshape(NZ, 8, COLS).astype(BF16)

    @pl.loop(1, NZ)
    def _(d):
        to = wrap(z + d, NZ)
        push(prsend.at[to], prbuf.at[z], pr_s.at[d], pr_r.at[z], dev(to, y, x, c))

    def add_share(d, total):
        frm = wrap(z - d + NZ, NZ)
        got(prbuf.at[frm], pr_r.at[frm])
        return total + prbuf[frm].astype(F32)

    hidden = lax.fori_loop(
        1, NZ, add_share, res_ref[...].astype(F32) + prsend[z].astype(F32)
    )
    hsend[...] = (hidden * gain_ref[v]).astype(BF16)

    half, low = z // 8, z % 8

    @pl.loop(1, NZ)
    def _(d):
        to = wrap(z + d, NZ)
        push(hsend, hall.at[y, x, low, c], h_s.at[d], h_r.at[low, c], dev(to, y, x, half))

    @pl.when(c == half)
    def _():
        keep = pltpu.make_async_copy(hsend, hall.at[y, x, low, c], h_r.at[low, c])
        keep.start()

    @pl.when(c != half)
    def _():
        push(hsend, hall.at[y, x, low, c], h_s.at[0], h_r.at[low, c], dev(z, y, x, half))

    @pl.loop(0, 8)
    def _(j):
        for cc in range(NC):
            got(hall.at[y, x, j, cc], h_r.at[j, cc])

    for d in range(1, 4):
        first = hall.at[y, x, pl.ds(0, 4)]
        push(first, first, h1_s.at[0, d], h1_r.at[0, x], dev(z, y, wrap(x + d, NX), c))
        second = hall.at[y, x, pl.ds(4, 4)]
        push(second, second, h1_s.at[1, d], h1_r.at[1, y], dev(z, wrap(y + d, NY), x, c))

    for e in range(4):
        xx, yy = wrap(x + e, NX), wrap(y + e, NY)
        first = hall.at[y, xx, pl.ds(0, 4)]
        second = hall.at[yy, x, pl.ds(4, 4)]
        if e > 0:
            got(first, h1_r.at[0, xx])
            got(second, h1_r.at[1, yy])
        for d in range(1, 4):
            push(first, first, h2_s.at[0, e, d], h2_r.at[0, y, xx], dev(z, wrap(y + d, NY), x, c))
            push(second, second, h2_s.at[1, e, d], h2_r.at[1, x, yy], dev(z, y, wrap(x + d, NX), c))

    own_head.wait()
    got(whead.at[1], hw_r.at[0])
    for d in range(1, 4):
        frm_y, frm_x = wrap(y + d, NY), wrap(x + d, NX)
        for e in range(4):
            got(hall.at[frm_y, e, pl.ds(0, 4)], h2_r.at[0, frm_y, e])
            got(hall.at[e, frm_x, pl.ds(4, 4)], h2_r.at[1, frm_x, e])

    logit[...] = jnp.zeros_like(logit)

    def head_step(n, squares):
        hid = hall[:, n // 2, :, n % 2].astype(F32).reshape(256, COLS)
        squares = squares + nt(ginv_ref[n], hid * hid, lax.Precision.HIGHEST)
        hid16 = hid.astype(BF16)
        cols = pl.ds(pl.multiple_of(n * COLS, 128), COLS)
        for p in range(2):
            logit[p] += nt(whead[p, :, cols], hid16)
        return squares

    squares = lax.fori_loop(0, NV, head_step, jnp.zeros((8, 256), F32))
    row_scale = lax.rsqrt(squares[0:1] / WIDTH + FLOOR)
    targets = tgt_ref[c]
    row_id = lax.broadcasted_iota(jnp.int32, (ROWS, 256), 0)
    tops, parts, picks = [], [], []
    for p in range(2):
        block = s * NV + (v if p == 0 else v + 1 - 2 * c)
        lg = logit[p] * row_scale
        logit[p] = lg
        picks.append(
            jnp.sum(jnp.where(row_id == targets - block * ROWS, lg, 0.0), axis=0, keepdims=True)
        )
        tops.append(jnp.max(lg, axis=0, keepdims=True))
    top = jnp.maximum(tops[0], tops[1])
    for p in range(2):
        parts.append(jnp.sum(jnp.exp(logit[p] - top), axis=0, keepdims=True))
    stsrc[...] = jnp.concatenate(
        [top, parts[0] + parts[1], picks[0] + picks[1], jnp.zeros((5, 256), F32)], axis=0
    )

    def join(one, two):
        m = jnp.maximum(one[0:1], two[0:1])
        t = one[1:2] * jnp.exp(one[0:1] - m) + two[1:2] * jnp.exp(two[0:1] - m)
        return jnp.concatenate([m, t, one[2:3] + two[2:3], one[3:8]], axis=0)

    q = y * NX + x

    @pl.loop(1, 16)
    def _(k):
        o = wrap(q + k, 16)
        push(stsrc, stbuf.at[q], t1_s.at[k], t1_r.at[q], dev(z, o // NX, o % NX, c))

    def join_plane(k, state):
        frm = wrap(q - k + 16, 16)
        got(stbuf.at[frm], t1_r.at[frm])
        return join(state, stbuf[frm])

    plane = lax.fori_loop(1, 16, join_plane, stsrc[...])
    stplane[0] = plane[:, 0:128]
    stplane[1] = plane[:, 128:256]

    side = y // 2

    @pl.loop(0, 8)
    def _(j):
        to = 8 * c + j

        @pl.when(to != z)
        def _():
            for cc in range(NC):
                push(stplane.at[side], stz.at[z], t2_s.at[j, cc], t2_r.at[z], dev(to, y, x, cc))

        @pl.when(to == z)
        def _():
            push(stplane.at[side], stz.at[z], t2_s.at[j, 0], t2_r.at[z], dev(z, y, x, 1 - c))
            keep = pltpu.make_async_copy(stplane.at[side], stz.at[z], t2_r.at[z])
            keep.start()

    @pl.loop(0, NZ)
    def _(j):
        got(stz.at[j], t2_r.at[j])

    final = stz[0]
    for j in range(1, NZ):
        final = join(final, stz[j])
    logprob = final[2:3] - final[0:1] - jnp.log(final[1:2])
    shift = lax.rem(128 - ((y % 2) * 64 + (z % 8) * 8), 128)
    out_ref[...] = pltpu.roll(jnp.broadcast_to(logprob, (8, 128)), shift, 1)

    @pl.loop(1, NZ)
    def _(d):
        got(q1src.at[0], q1_s.at[d])
        got(prsend.at[0], pr_s.at[d])
        got(hsend, h_s.at[d])

    @pl.when(c != half)
    def _():
        got(hsend, h_s.at[0])

    @pl.loop(1, 8)
    def _(d):
        got(kvbuf.at[0, 0, 0], kv_s.at[d, 0])
        got(kvbuf.at[0, 0, 1], kv_s.at[d, 1])
        got(qall.at[0], qa_s.at[d])
        got(osend.at[0], o_s.at[d])
        got(abuf.at[0], a_s.at[d])

    for e in range(1, NY):
        got(wbuf.at[0], w_s.at[e])

        @pl.loop(0, 8)
        def _(j):
            got(kvbuf.at[0, 0], kf_s.at[j, e])

    got(whead.at[1], hw_s.at[0])
    got(psrc, p_s.at[0])
    for d in range(1, 4):
        for i in range(2):
            got(hall.at[0, 0, pl.ds(0, 4)], h1_s.at[i, d])
            for e in range(4):
                got(hall.at[0, 0, pl.ds(0, 4)], h2_s.at[i, e, d])

    @pl.loop(1, 16)
    def _(k):
        got(stsrc, t1_s.at[k])

    @pl.loop(0, 8)
    def _(j):
        got(stplane.at[0], t2_s.at[j, 0])

        @pl.when(8 * c + j != z)
        def _():
            got(stplane.at[0], t2_s.at[j, 1])


def body(
    queries,
    cached_keys,
    cached_values,
    out_weight,
    residual,
    norm_gain,
    head_weight,
    targets,
    span_offset,
):
    gain = norm_gain.astype(F32).reshape(NV, 1, COLS)
    gain_inv = jnp.broadcast_to(1.0 / (gain * gain), (NV, 8, COLS))
    tgt = targets.reshape(2, 8, NY, 8).transpose(0, 2, 1, 3).reshape(2, 1, 256)
    vm = pl.BlockSpec(memory_space=pltpu.VMEM)
    hbm = pl.BlockSpec(memory_space=pl.ANY)
    dma = pltpu.SemaphoreType.DMA
    out = pl.pallas_call(
        kernel,
        out_shape=jax.ShapeDtypeStruct((8, 128), F32),
        in_specs=[pl.BlockSpec(memory_space=pltpu.SMEM), vm, hbm, hbm, hbm, vm, vm, vm, hbm, vm],
        out_specs=vm,
        scratch_shapes=[
            pltpu.VMEM((8, 8, 128), F32),
            pltpu.VMEM((NZ, 8, 128), F32),
            pltpu.VMEM((NV, 128, 128), BF16),
            pltpu.VMEM((NY, 8, 2, 64, 128), BF16),
            pltpu.VMEM((128, 2048), BF16),
            pltpu.VMEM((NY, 512, 128), F32),
            pltpu.VMEM((NV, 144, 128), BF16),
            pltpu.VMEM((NV, 144, 128), BF16),
            pltpu.VMEM((144, 128), BF16),
            pltpu.VMEM((144, 128), BF16),
            pltpu.VMEM((128, 128), BF16),
            pltpu.VMEM((NV, 64, 128), BF16),
            pltpu.VMEM((NY, 128, COLS), BF16),
            pltpu.VMEM((NZ, 8, COLS), BF16),
            pltpu.VMEM((NZ, 8, COLS), BF16),
            pltpu.VMEM((8, COLS), BF16),
            pltpu.VMEM((NY, NX, 8, NC, 8, COLS), BF16),
            pltpu.VMEM((2, ROWS, WIDTH), BF16),
            pltpu.VMEM((2, ROWS, 256), F32),
            pltpu.VMEM((8, 256), F32),
            pltpu.VMEM((16, 8, 256), F32),
            pltpu.VMEM((2, 8, 128), F32),
            pltpu.VMEM((NZ, 8, 128), F32),
            dma((8, 2)),
            dma((8, 2)),
            dma((NZ,)),
            dma((NZ,)),
            dma((8, NY)),
            dma((NY, 8)),
            dma((NV,)),
            dma((NV,)),
            dma((NV,)),
            dma((NV,)),
            dma((1,)),
            dma((1,)),
            dma((NV,)),
            dma((NV,)),
            dma((NY,)),
            dma((NY,)),
            dma((NZ,)),
            dma((NZ,)),
            dma((NZ,)),
            dma((8, NC)),
            dma((2, 4)),
            dma((2, 4)),
            dma((2, 4, 4)),
            dma((2, 4, 4)),
            dma((1,)),
            dma((1,)),
            dma((16,)),
            dma((16,)),
            dma((8, NC)),
            dma((NZ,)),
            dma((4,)),
        ],
        compiler_params=pltpu.CompilerParams(
            collective_id=0, has_side_effects=True, vmem_limit_bytes=48 * 2**20
        ),
        cost_estimate=pl.CostEstimate(
            flops=3_000_000_000, bytes_accessed=8_000_000, transcendentals=2_500_000
        ),
    )(
        span_offset,
        queries,
        cached_keys,
        cached_values,
        out_weight,
        residual,
        gain,
        gain_inv,
        head_weight,
        tgt,
    )
    return out[0, :8]


def solution(mesh):
    return jax.shard_map(
        body,
        mesh=mesh,
        in_specs=(
            P("seq", None),
            P(("seq", "vocab"), None),
            P(("seq", "vocab"), None),
            P("seq", "vocab"),
            P("seq", "vocab"),
            P(),
            P(("seq", "vocab"), None),
            P(),
            P(),
        ),
        out_specs=P("seq"),
        check_vma=False,
    )
```

profile of v0, /device:TPU:1, one launch (start us, length us, event | category | flops | bytes accessed | tf_op | source)
XLA Modules:
  0.0 136.0 jit_solution(14550439687565757393)
XLA Ops:
  0.7 0.7 multiply_divide_fusion
  1.4 0.7 convert_element_type.3
  2.1 0.8 reshape.22
  2.9 0.1 reshape.23.tgt_ref
  3.0 0.0 copy-start
  3.0 1.8 %copy-done = bf16[296,5120]{1,0:T(8,128)(2,1)S(1)} copy-done((bf16[296,5120]{1,0:T(8,128)(2,1)S(1)}, bf16[296,5120]{1,0:T(8,128)(2,1)}, u32[]{:S(2)}) %copy-start) | copy-done | bytes 3031064
  4.8 0.0 copy-start.1
  4.8 0.9 copy-done.1
  5.8 0.0 copy-start.2
  5.8 0.9 copy-done.2
  6.7 0.0 copy-start.3
  6.7 0.9 copy-done.3
  7.6 0.0 copy-start.4
  7.6 0.9 copy-done.4
  8.5 0.0 copy-start.5
  8.5 0.7 copy-done.5
  9.2 126.3 %shard_map.91 = f32[8,128]{1,0:T(8,128)S(1)} custom-call(s32[1]{0:T(128)S(6)} %copy.11.span_ref, bf16[8,8192]{1,0:T(8,128)(2,1)S(1)} %copy-done.2, bf16[64,1024]{1,0:T(8,128)(2,1)S(1)} %copy-done.3, bf16[64,1024]{1,0:T(8,128)(2,1)S(1)} %copy-done.4, bf16[128,640]{1,0:T(8,128)(2,1)S(1)} %copy-done.1, bf16[8,640]{1,0:T(8,128)(2,1)S(1)} %copy-done.5, ...), custom_call_target="tpu_custom_call" | custom-call | flops 3000000000 | bytes 8000000 | tf_op jit(solution)/shard_map/pallas_call | solution.py:536
  135.5 0.5 slice_bitcast_fusion
  (3 shorter events, 0.0 us)
Async XLA Ops:
  3.0 1.9 %copy-start = (bf16[296,5120]{1,0:T(8,128)(2,1)S(1)}, bf16[296,5120]{1,0:T(8,128)(2,1)}, u32[]{:S(2)}) copy-start(bf16[296,5120]{1,0:T(8,128)(2,1)} %head_ref.1) | copy-start | bytes 9093124
  4.8 0.9 copy-start.1
  5.8 0.9 copy-start.2
  6.7 0.9 copy-start.3
  7.6 0.9 copy-start.4
  8.5 0.7 copy-start.5
where the time goes:
time: 136 us
  Pallas kernels  126 us (93%)
  local copies, waits for them, and re-layouts  7.58 us (6%)
  other arithmetic  1.42 us (1%)
    pallas_call x1, Pallas kernels, body(): pl.pallas_call(kernel, out_shape=jax.ShapeDtypeStruct((8, 128), F32), in_...  126 us
    unnamed x12, local copies, waits for them, and re-layouts  6.18 us

commit v1 on v0

v1 whole, which is shorter than its diff:
```python
import math

import jax
import jax.numpy as jnp
from jax import lax
from jax.experimental import pallas as pl
from jax.experimental.pallas import tpu as pltpu
from jax.sharding import PartitionSpec as P

MESH = pl.DeviceIdType.MESH
HEAD_DIM = 128
NZ, NY, NX, NC = 16, 4, 4, 2
NV = NX * NC
WIDTH = 5120
COLS = WIDTH // NV
ROWS = 296
FLOOR = 1e-06
LOW = -1e30
F32 = jnp.float32
BF16 = jnp.bfloat16


def split3(x):
    hi = x.astype(BF16).astype(F32)
    rest = x - hi
    mid = rest.astype(BF16).astype(F32)
    lo = (rest - mid).astype(BF16).astype(F32)
    return hi, mid, lo


def nt(a, b, precision=None):
    return lax.dot_general(
        a, b, (((1,), (1,)), ((), ())), preferred_element_type=F32, precision=precision
    )


def kernel(
    span_ref,
    q_ref,
    k_ref,
    v_ref,
    w_ref,
    res_ref,
    gain_ref,
    head_ref,
    tgt_ref,
    out_ref,
    span_m,
    q_m,
    res_m,
    gain_m,
    tgt_m,
    gain_n,
    ginv_n,
    tgt_n,
    diff,
    q1src,
    q1buf,
    qall,
    kbuf,
    vbuf,
    wts_m,
    acc_m,
    run_m,
    osend,
    obuf,
    psrc,
    pbuf,
    att,
    abuf,
    wbuf,
    prsend,
    prbuf,
    hsend,
    hall,
    whead,
    logit,
    stsrc,
    stz,
    stred,
    stfin,
    kv_s,
    kv_r,
    kf_s,
    vf_s,
    kf_r,
    vf_r,
    q1_s,
    q1_r,
    qa_s,
    qa_r,
    o_s,
    o_r,
    p_s,
    p_r,
    a_s,
    a_r,
    w_s,
    w_r,
    wf_s,
    pr_s,
    pr_r,
    h_s,
    h_r,
    h1_s,
    h1_r,
    h2_s,
    h2_r,
    hw_s,
    hw_r,
    t1_s,
    t1_r,
    t2_s,
    t2_r,
    loc,
):
    s = lax.axis_index("seq")
    v = lax.axis_index("vocab")
    z, y, x, c = s // NY, s % NY, v // NC, v % NC
    g, par = z // 2, z % 2
    q = y * NX + x

    def dev(zz, yy, xx, cc):
        return (zz * NY + yy, xx * NC + cc)

    def wrap(a, n):
        return lax.rem(a + n, n)

    def flip(a, k):
        swaps = (a, a + 1 - 2 * lax.rem(a, 2), lax.rem(a + 2, 4), 3 - a)
        if isinstance(k, int):
            return swaps[k]
        return jnp.where(
            k < 2, jnp.where(k == 0, swaps[0], swaps[1]), jnp.where(k == 2, swaps[2], swaps[3])
        )

    def push(src, dst, ss, rs, to):
        cp = pltpu.make_async_remote_copy(
            src_ref=src, dst_ref=dst, send_sem=ss, recv_sem=rs, device_id=to, device_id_type=MESH
        )
        cp.start()

    def got(ref, sem):
        pltpu.make_async_copy(ref, ref, sem).wait()

    own_head = pltpu.make_async_copy(head_ref, whead.at[0], loc.at[0])
    own_head.start()
    own_w = pltpu.make_async_copy(w_ref, wbuf.at[par, y], loc.at[1])
    own_w.start()
    own_k = pltpu.make_async_copy(
        k_ref.at[:, pl.ds(pl.multiple_of(g * 128, 128), 128)], kbuf.at[y, 0], loc.at[2]
    )
    own_k.start()
    own_v = pltpu.make_async_copy(
        v_ref.at[:, pl.ds(pl.multiple_of(g * 128, 128), 128)], vbuf.at[y, 0], loc.at[3]
    )
    own_v.start()
    loads = [
        pltpu.make_async_copy(a, b, loc.at[4 + i])
        for i, (a, b) in enumerate(
            (
                (q_ref, q_m),
                (gain_ref, gain_m),
                (tgt_ref, tgt_m),
                (span_ref, span_m),
                (res_ref, res_m),
            )
        )
    ]
    for cp in loads:
        cp.start()

    barrier = pltpu.get_barrier_semaphore()

    def greet(zz, yy, xx, cc):
        pl.semaphore_signal(barrier, inc=1, device_id=dev(zz, yy, xx, cc), device_id_type=MESH)

    @pl.loop(1, NZ)
    def _(d):
        greet(wrap(z + d, NZ), y, x, c)
        greet(wrap(z + d, NZ), y, x, 1 - c)

    greet(z, y, x, 1 - c)
    for k in range(1, 16):
        for cc in range(NC):
            greet(z, flip(y, k // 4), flip(x, k % 4), cc)

    for cp in loads:
        cp.wait()
    q_f = q_m[...].astype(F32)
    pick_row = lax.broadcasted_iota(jnp.int32, (8, 128), 0) == v
    for gg in range(8):
        rows = []
        for h in range(8 * gg, 8 * gg + 8):
            part = jnp.where(pick_row, q_f[:, h * 128 : (h + 1) * 128], 0.0)
            rows.append(jnp.sum(part, axis=0, keepdims=True))
        q1src[gg] = jnp.concatenate(rows, axis=0).astype(BF16)

    pl.semaphore_wait(barrier, 2 * (NZ - 1) + 31)

    @pl.loop(1, NZ)
    def _(d):
        to = wrap(z + d, NZ)
        push(q1src.at[to // 2], q1buf.at[z], q1_s.at[d], q1_r.at[z], dev(to, y, x, c))

    def spread(src, dst, i):
        @pl.loop(1, 8)
        def _(d):
            head = wrap(g + d, 8)
            ahead = 2 * d - par
            up = ahead <= 7
            to = dev(2 * head + jnp.where(up, 0, 1), y, x, c)
            k = jnp.where(up, ahead, 15 - ahead)
            cols = pl.ds(pl.multiple_of(head * 128, 128), 128)
            push(src.at[:, cols], dst.at[y, k], kv_s.at[d, i], kv_r.at[k, i], to)

    spread(k_ref, kbuf, 0)
    spread(v_ref, vbuf, 1)

    for d in range(1, NY):
        push(w_ref, wbuf.at[par, y], w_s.at[d], w_r.at[par, y], dev(z, wrap(y + d, NY), x, c))
    push(head_ref, whead.at[1], hw_s.at[0], hw_r.at[0], dev(z, y, x, 1 - c))

    gains = gain_m[...].astype(F32).reshape(WIDTH // 128, 128)
    for t in range(WIDTH // 128):
        one = gains[t : t + 1]
        lanes = slice((t % 5) * 128, (t % 5 + 1) * 128)
        gain_n[t // 5, :, lanes] = one
        ginv_n[t // 5, :, lanes] = jnp.broadcast_to(1.0 / (one * one), (8, 128))
    tgt4 = tgt_m[...].reshape(4, 128).astype(F32)
    src = lax.broadcasted_iota(jnp.int32, (128, 256), 0)
    dst = lax.broadcasted_iota(jnp.int32, (128, 256), 1)
    plane_of = lax.rem(dst // 32 + z, 8)
    here = src == (plane_of % 4) * 32 + dst % 32
    ordered = jnp.zeros((8, 256), F32)
    for r in range(2):
        row = jnp.where(c == 0, tgt4[r : r + 1], tgt4[2 + r : 3 + r])
        ordered = ordered + jnp.dot(
            jnp.broadcast_to(row, (8, 128)),
            jnp.where(here & (plane_of // 4 == r), 1.0, 0.0),
            preferred_element_type=F32,
            precision=lax.Precision.HIGHEST,
        )
    tgt_n[...] = ordered.astype(jnp.int32)

    rho = lax.broadcasted_iota(jnp.int32, (512, 512), 0)
    lane = lax.broadcasted_iota(jnp.int32, (512, 512), 1)
    slot = rho // 64
    plane_k = jnp.bitwise_and(jnp.where(par == 0, z - slot, z + slot), 15)
    pos = plane_k * 2048 + v * 64 + rho % 64
    diff[...] = pos - (32 * (2 * (lane % 8) + (lane // 64) % 2) + lane // 128)

    q1buf[z] = q1src[g]

    @pl.loop(1, NZ)
    def _(d):
        frm = wrap(z - d + NZ, NZ)
        got(q1buf.at[frm], q1_r.at[frm])

    ri = lax.broadcasted_iota(jnp.int32, (128, 128), 0)
    ci = lax.broadcasted_iota(jnp.int32, (128, 128), 1)
    from_row = (2 * (ri % 8) + ri // 64) * 8 + (ri // 8) % 8
    q_rows = q1buf[...].astype(F32).reshape(128, 128).astype(BF16)
    qall[v] = jnp.dot(
        (ci == from_row).astype(BF16), q_rows, preferred_element_type=F32
    ).astype(BF16)

    @pl.loop(1, NV)
    def _(k):
        o = wrap(v + k, NV)
        push(qall.at[v], qall.at[v], qa_s.at[k], qa_r.at[v], dev(z, y, o // NC, o % NC))

    def forward(buf, i, ss, rs):
        @pl.loop(0, 8)
        def _(k):
            @pl.when(k > 0)
            def _():
                got(buf.at[y, k], kv_r.at[k, i])

            for e in (1, 3, 2):
                to = dev(z, wrap(y + e, NY), x, c)
                push(buf.at[y, k], buf.at[y, k], ss.at[k, e], rs.at[y, k], to)

    own_k.wait()
    forward(kbuf, 0, kf_s, kf_r)

    @pl.loop(1, NV)
    def _(k):
        o = wrap(v + k, NV)
        got(qall.at[o], qa_r.at[o])

    span = span_m[0]
    turn = math.log2(math.e) / math.sqrt(HEAD_DIM)

    def stat_rows(top, total):
        rows = list(split3(top)) + list(split3(total))
        return jnp.concatenate(rows + [jnp.zeros((10, top.shape[1]), F32)], axis=0).astype(BF16)

    def weigh(e):
        yy = wrap(y - e + NY, NY)
        keys = kbuf[yy].reshape(512, 128)
        for i in range(2):
            scores = nt(keys, qall[4 * i : 4 * i + 4].reshape(512, 128))
            live = diff[...] <= span + 8 * y + 4 * i - 512 * yy
            scores = jnp.where(live, scores, LOW)
            top = jnp.maximum(jnp.max(scores, axis=0, keepdims=True), 0.5 * LOW)
            wts = jnp.exp2((scores - top) * turn)
            run_m[i, e, 0:1] = top
            run_m[i, e, 1:2] = jnp.sum(wts, axis=0, keepdims=True)
            wts_m[i, e] = wts.astype(BF16)

    def mix(e):
        yy = wrap(y - e + NY, NY)
        vals_t = vbuf[yy].reshape(512, 128).T
        for i in range(2):
            tops = [run_m[i, b, 0:1] for b in range(NY)]
            top = jnp.maximum(jnp.maximum(tops[0], tops[1]), jnp.maximum(tops[2], tops[3]))
            acc = jnp.dot(vals_t, wts_m[i, e], preferred_element_type=F32)
            acc = acc * jnp.exp2((tops[e] - top) * turn)
            if e > 0:
                acc = acc + acc_m[i]
            if e < NY - 1:
                acc_m[i] = acc
                continue
            total = jnp.zeros((1, 512), F32)
            for b in range(NY):
                total = total + run_m[i, b, 1:2] * jnp.exp2((tops[b] - top) * turn)
            tail = stat_rows(top, total)
            for b in range(4):
                o = 4 * i + b
                lanes = slice(b * 128, (b + 1) * 128)
                osend[o, 0:128, :] = acc[:, lanes].astype(BF16)
                osend[o, 128:144, :] = tail[:, lanes]

                @pl.when(v != o)
                def _():
                    push(osend.at[o], obuf.at[v], o_s.at[o], o_r.at[v], dev(z, y, o // NC, o % NC))

    def arrived(e, buf, rs):
        yy = wrap(y - e + NY, NY)

        @pl.loop(0, 8)
        def _(k):
            got(buf.at[yy, k], rs.at[yy, k])

    weigh(0)
    own_v.wait()
    forward(vbuf, 1, vf_s, vf_r)
    own_w.wait()
    push(wbuf.at[par, y], wbuf.at[par, y], w_s.at[0], w_r.at[par, y], dev(z + 1 - 2 * par, y, x, c))
    for e in (1, 3, 2):
        arrived(e, kbuf, kf_r)
        weigh(e)
    mix(0)
    for e in (1, 2, 3):
        arrived(e, vbuf, vf_r)
        mix(e)

    got(wbuf.at[1 - par, y], w_r.at[1 - par, y])
    for d in range(1, NY):
        there = wbuf.at[1 - par, y]
        push(there, there, wf_s.at[d], w_r.at[1 - par, y], dev(z, wrap(y + d, NY), x, c))

    def unpack_stats(tail):
        b = tail.astype(F32)
        return b[0:1] + b[1:2] + b[2:3], b[3:4] + b[4:5] + b[5:6]

    def blend(one, two):
        m1, l1, a1 = one
        m2, l2, a2 = two
        m = jnp.maximum(m1, m2)
        f1, f2 = jnp.exp2((m1 - m) * turn), jnp.exp2((m2 - m) * turn)
        return m, l1 * f1 + l2 * f2, a1 * f1 + a2 * f2

    obuf[v] = osend[v]

    @pl.loop(1, NV)
    def _(k):
        frm = wrap(v - k + NV, NV)
        got(obuf.at[frm], o_r.at[frm])

    tails = [unpack_stats(obuf[i, 128:144, :]) for i in range(NV)]
    m_own = tails[0][0]
    for m_one, _ in tails[1:]:
        m_own = jnp.maximum(m_own, m_one)
    l_own = jnp.zeros((1, 128), F32)
    a_own = jnp.zeros((128, 128), F32)
    for i, (m_one, l_one) in enumerate(tails):
        fade = jnp.exp2((m_one - m_own) * turn)
        l_own = l_own + l_one * fade
        a_own = a_own + obuf[i, 0:128, :].astype(F32) * fade

    psrc[0:128, :] = a_own.astype(BF16)
    psrc[128:144, :] = stat_rows(m_own, l_own)
    push(psrc, pbuf, p_s.at[0], p_r.at[0], dev(z + 1 - 2 * par, y, x, c))
    got(pbuf, p_r.at[0])
    m_two, l_two = unpack_stats(pbuf[128:144, :])
    _, l_all, a_all = blend(
        (m_own, l_own, a_own), (m_two, l_two, pbuf[0:128, :].astype(F32))
    )
    att[...] = (a_all / l_all).T.astype(BF16)

    mine = att.at[pl.ds(pl.multiple_of(par * 64, 64), 64)]

    @pl.loop(1, NV)
    def _(k):
        o = wrap(v + k, NV)
        push(mine, abuf.at[v], a_s.at[k], a_r.at[v], dev(z, y, o // NC, o % NC))

    abuf[v] = att[pl.ds(pl.multiple_of(par * 64, 64), 64), :]
    for d in range(1, NY):
        frm_y = wrap(y - d + NY, NY)
        got(wbuf.at[par, frm_y], w_r.at[par, frm_y])
        got(wbuf.at[1 - par, frm_y], w_r.at[1 - par, frm_y])

    @pl.loop(1, NV)
    def _(k):
        frm = wrap(v - k + NV, NV)
        got(abuf.at[frm], a_r.at[frm])

    rows_f = abuf[...].astype(F32)
    proj = jnp.zeros((64, COLS), F32)
    for h in range(8):
        rows = rows_f[:, h * 8 : (h + 1) * 8, :].reshape(64, 128).astype(BF16)
        proj = proj + jnp.dot(rows, wbuf[h // 4, h % 4], preferred_element_type=F32)
    r64 = lax.broadcasted_iota(jnp.int32, (64, 64), 0)
    c64 = lax.broadcasted_iota(jnp.int32, (64, 64), 1)
    to_planes = (c64 == (r64 % 8) * 8 + r64 // 8).astype(BF16)
    by_plane = jnp.dot(to_planes, proj.astype(BF16), preferred_element_type=F32)
    prsend[...] = by_plane.reshape(8, 8, COLS).astype(BF16)

    @pl.loop(1, 8)
    def _(d):
        to = wrap(g + d, 8)
        push(prsend.at[to], prbuf.at[g], pr_s.at[d], pr_r.at[g], dev(2 * to + par, y, x, c))

    hidden = res_m[...].astype(F32) + prsend[g].astype(F32)
    for d in range(1, 8):
        frm = wrap(g - d + 8, 8)
        got(prbuf.at[frm], pr_r.at[frm])
        hidden = hidden + prbuf[frm].astype(F32)
    hsend[...] = (hidden * gain_n[v]).astype(BF16)

    half = z // 8

    @pl.loop(1, NZ)
    def _(d):
        to = wrap(z + d, NZ)
        k = lax.rem(z + 16 - to, 8)
        push(hsend, hall.at[x, k, y, c], h_s.at[d], h_r.at[k, c], dev(to, y, x, half))

    @pl.when(c == half)
    def _():
        keep = pltpu.make_async_copy(hsend, hall.at[x, 0, y, c], h_r.at[0, c])
        keep.start()

    @pl.when(c != half)
    def _():
        push(hsend, hall.at[x, 0, y, c], h_s.at[0], h_r.at[0, c], dev(z, y, x, half))

    def block(xx, yy, i):
        return hall.at[xx, pl.ds(2 * i, 2), yy]

    def first_step(i, x_first):
        for k in (2 * i, 2 * i + 1):
            for cc in range(NC):
                got(hall.at[x, k, y, cc], h_r.at[k, cc])
        for d in (1, 3, 2):
            to = dev(z, y, wrap(x + d, NX), c) if x_first else dev(z, wrap(y + d, NY), x, c)
            here = x if x_first else y
            push(block(x, y, i), block(x, y, i), h1_s.at[i, d], h1_r.at[i, here], to)

    def second_step(i, x_first):
        for e in (0, 1, 3, 2):
            xx = wrap(x + e, NX) if x_first else x
            yy = y if x_first else wrap(y + e, NY)
            there, here = (xx, y) if x_first else (yy, x)
            if e > 0:
                got(block(xx, yy, i), h1_r.at[i, there])
            for d in (1, 3, 2):
                to = dev(z, wrap(y + d, NY), x, c) if x_first else dev(z, y, wrap(x + d, NX), c)
                push(
                    block(xx, yy, i),
                    block(xx, yy, i),
                    h2_s.at[i, e, d],
                    h2_r.at[i, here, there],
                    to,
                )

    def arrivals(i, x_first):
        for d in range(1, 4):
            for e in range(4):
                frm = wrap((y if x_first else x) + d, 4)
                xx, yy = (e, frm) if x_first else (frm, e)
                got(block(xx, yy, i), h2_r.at[i, frm, e])

    first_step(0, True)
    first_step(3, False)
    second_step(0, True)
    first_step(1, True)
    second_step(3, False)
    first_step(2, False)
    second_step(1, True)
    second_step(2, False)

    own_head.wait()
    got(whead.at[1], hw_r.at[0])
    for i, x_first in ((0, True), (3, False), (1, True), (2, False)):
        arrivals(i, x_first)

    logit[...] = jnp.zeros_like(logit)

    def head_step(n, squares):
        hid = hall[n // 2, :, :, lax.rem(n, 2)].astype(F32).reshape(256, COLS)
        inv = ginv_n[n]
        for t in range(COLS // 128):
            part = hid[:, t * 128 : (t + 1) * 128]
            squares = squares + part * part * inv[0:1, t * 128 : (t + 1) * 128]
        hid16 = hid.astype(BF16)
        cols = pl.ds(pl.multiple_of(n * COLS, 128), COLS)
        for p in range(2):
            logit[p] += nt(whead[p, :, cols], hid16)
        return squares

    squares = lax.fori_loop(0, NV, head_step, jnp.zeros((256, 128), F32))
    sums = nt(jnp.ones((8, 128), F32), squares, lax.Precision.HIGHEST)
    row_scale = lax.rsqrt(sums[0:1] / WIDTH + FLOOR)
    targets = tgt_n[0:1]
    row_id = lax.broadcasted_iota(jnp.int32, (ROWS, 256), 0)
    tops, parts, picks = [], [], []
    for p in range(2):
        block = s * NV + (v if p == 0 else v + 1 - 2 * c)
        lg = logit[p] * row_scale
        logit[p] = lg
        picks.append(
            jnp.sum(jnp.where(row_id == targets - block * ROWS, lg, 0.0), axis=0, keepdims=True)
        )
        tops.append(jnp.max(lg, axis=0, keepdims=True))
    top = jnp.maximum(tops[0], tops[1])
    for p in range(2):
        parts.append(jnp.sum(jnp.exp(logit[p] - top), axis=0, keepdims=True))
    stats = jnp.concatenate(
        [top, parts[0] + parts[1], picks[0] + picks[1], jnp.zeros((5, 256), F32)], axis=0
    )
    stsrc[...] = jnp.zeros_like(stsrc)
    for k in range(8):
        stsrc[k, :, 0:32] = stats[:, k * 32 : (k + 1) * 32]

    def join_all(ref, n):
        m = ref[0, 0:1]
        for i in range(1, n):
            m = jnp.maximum(m, ref[i, 0:1])
        t = jnp.zeros_like(m)
        picked = jnp.zeros_like(m)
        for i in range(n):
            t = t + ref[i, 1:2] * jnp.exp(ref[i, 0:1] - m)
            picked = picked + ref[i, 2:3]
        return m, t, picked

    @pl.loop(0, 8)
    def _(k):
        to = 8 * c + lax.rem(z + k, 8)

        @pl.when(to != z)
        def _():
            push(stsrc.at[k], stz.at[z], t1_s.at[k], t1_r.at[z], dev(to, y, x, c))

    @pl.when(c == half)
    def _():
        stz[z] = stsrc[0]

        @pl.loop(1, NZ)
        def _(d):
            frm = wrap(z + d, NZ)
            got(stz.at[frm], t1_r.at[frm])

        m, t, picked = join_all(stz, NZ)
        stred[...] = jnp.concatenate([m, t, picked, jnp.zeros((5, 128), F32)], axis=0)

        push(stred, stfin.at[q], t2_s.at[0, 0], t2_r.at[q], dev(z, y, x, 1 - c))
        for k in (1, 4, 3, 12, 2, 8, 5, 15, 6, 9, 7, 13, 10, 11, 14):
            for cc in range(NC):
                to = dev(z, flip(y, k // 4), flip(x, k % 4), cc)
                push(stred, stfin.at[q], t2_s.at[k, cc], t2_r.at[q], to)
        stfin[q] = stred[...]

    @pl.when(c != half)
    def _():
        got(stfin.at[q], t2_r.at[q])

    for k in range(1, 16):
        o = flip(y, k // 4) * NX + flip(x, k % 4)
        got(stfin.at[o], t2_r.at[o])

    m, t, picked = join_all(stfin, 16)
    logprob = picked - m - jnp.log(t)
    shift = lax.rem(128 - y * 8, 128)
    out_ref[...] = pltpu.roll(jnp.broadcast_to(logprob, (8, 128)), shift, 1)

    @pl.loop(1, NZ)
    def _(d):
        got(q1src.at[0], q1_s.at[d])
        got(hsend, h_s.at[d])

    @pl.when(c != half)
    def _():
        got(hsend, h_s.at[0])

    @pl.loop(1, 8)
    def _(d):
        got(kbuf.at[0, 0], kv_s.at[d, 0])
        got(vbuf.at[0, 0], kv_s.at[d, 1])
        got(qall.at[0], qa_s.at[d])
        got(prsend.at[0], pr_s.at[d])
        got(abuf.at[0], a_s.at[d])

    @pl.loop(0, NV)
    def _(o):
        @pl.when(o != v)
        def _():
            got(osend.at[0], o_s.at[o])

    got(wbuf.at[0, 0], w_s.at[0])
    for d in range(1, NY):
        got(wbuf.at[0, 0], w_s.at[d])
        got(wbuf.at[0, 0], wf_s.at[d])

        @pl.loop(0, 8)
        def _(k):
            got(kbuf.at[0, 0], kf_s.at[k, d])
            got(vbuf.at[0, 0], vf_s.at[k, d])

    got(whead.at[1], hw_s.at[0])
    got(psrc, p_s.at[0])

    @pl.loop(0, 4)
    def _(i):
        for d in range(1, 4):
            got(hall.at[0, pl.ds(0, 2), 0], h1_s.at[i, d])
            for e in range(4):
                got(hall.at[0, pl.ds(0, 2), 0], h2_s.at[i, e, d])

    @pl.loop(0, 8)
    def _(k):
        @pl.when(8 * c + lax.rem(z + k, 8) != z)
        def _():
            got(stsrc.at[0], t1_s.at[k])

    @pl.when(c == half)
    def _():
        got(stred, t2_s.at[0, 0])

        @pl.loop(1, 16)
        def _(k):
            for cc in range(NC):
                got(stred, t2_s.at[k, cc])


def body(
    queries,
    cached_keys,
    cached_values,
    out_weight,
    residual,
    norm_gain,
    head_weight,
    targets,
    span_offset,
):
    vm = pl.BlockSpec(memory_space=pltpu.VMEM)
    hbm = pl.BlockSpec(memory_space=pl.ANY)
    dma = pltpu.SemaphoreType.DMA
    out = pl.pallas_call(
        kernel,
        out_shape=jax.ShapeDtypeStruct((8, 128), F32),
        in_specs=[hbm] * 9,
        out_specs=vm,
        scratch_shapes=[
            pltpu.SMEM((1,), jnp.int32),
            pltpu.VMEM((8, 64 * HEAD_DIM), BF16),
            pltpu.VMEM((8, COLS), BF16),
            pltpu.VMEM((WIDTH,), BF16),
            pltpu.VMEM((512,), jnp.int32),
            pltpu.VMEM((NV, 1, COLS), F32),
            pltpu.VMEM((NV, 8, COLS), F32),
            pltpu.VMEM((8, 256), jnp.int32),
            pltpu.VMEM((512, 512), jnp.int32),
            pltpu.VMEM((8, 8, 128), BF16),
            pltpu.VMEM((NZ, 8, 128), BF16),
            pltpu.VMEM((NV, 128, 128), BF16),
            pltpu.VMEM((NY, 8, 64, 128), BF16),
            pltpu.VMEM((NY, 8, 64, 128), BF16),
            pltpu.VMEM((2, NY, 512, 512), BF16),
            pltpu.VMEM((2, 128, 512), F32),
            pltpu.VMEM((2, NY, 8, 512), F32),
            pltpu.VMEM((NV, 144, 128), BF16),
            pltpu.VMEM((NV, 144, 128), BF16),
            pltpu.VMEM((144, 128), BF16),
            pltpu.VMEM((144, 128), BF16),
            pltpu.VMEM((128, 128), BF16),
            pltpu.VMEM((NV, 64, 128), BF16),
            pltpu.VMEM((2, NY, 128, COLS), BF16),
            pltpu.VMEM((8, 8, COLS), BF16),
            pltpu.VMEM((8, 8, COLS), BF16),
            pltpu.VMEM((8, COLS), BF16),
            pltpu.VMEM((NX, 8, NY, NC, 8, COLS), BF16),
            pltpu.VMEM((2, ROWS, WIDTH), BF16),
            pltpu.VMEM((2, ROWS, 256), F32),
            pltpu.VMEM((8, 8, 128), F32),
            pltpu.VMEM((NZ, 8, 128), F32),
            pltpu.VMEM((8, 128), F32),
            pltpu.VMEM((16, 8, 128), F32),
            dma((8, 2)),
            dma((8, 2)),
            dma((8, NY)),
            dma((8, NY)),
            dma((NY, 8)),
            dma((NY, 8)),
            dma((NZ,)),
            dma((NZ,)),
            dma((NV,)),
            dma((NV,)),
            dma((NV,)),
            dma((NV,)),
            dma((1,)),
            dma((1,)),
            dma((NV,)),
            dma((NV,)),
            dma((NY,)),
            dma((2, NY)),
            dma((NY,)),
            dma((8,)),
            dma((8,)),
            dma((NZ,)),
            dma((8, NC)),
            dma((4, 4)),
            dma((4, 4)),
            dma((4, 4, 4)),
            dma((4, 4, 4)),
            dma((1,)),
            dma((1,)),
            dma((8,)),
            dma((NZ,)),
            dma((16, NC)),
            dma((16,)),
            dma((9,)),
        ],
        compiler_params=pltpu.CompilerParams(
            collective_id=0, has_side_effects=True, vmem_limit_bytes=60 * 2**20
        ),
        cost_estimate=pl.CostEstimate(
            flops=3_000_000_000, bytes_accessed=8_000_000, transcendentals=2_500_000
        ),
    )(
        span_offset,
        queries,
        cached_keys,
        cached_values,
        out_weight,
        residual,
        norm_gain,
        head_weight,
        targets,
    )
    return out[0, :8]


def solution(mesh):
    return jax.shard_map(
        body,
        mesh=mesh,
        in_specs=(
            P("seq", None),
            P(("seq", "vocab"), None),
            P(("seq", "vocab"), None),
            P("seq", "vocab"),
            P("seq", "vocab"),
            P(),
            P(("seq", "vocab"), None),
            P(),
            P(),
        ),
        out_specs=P("seq"),
        check_vma=False,
    )
```

time: 136 us -> 120 us (0.88)
  Pallas kernels: 126 us -> 118 us
  local copies, waits for them, and re-layouts: 7.58 us -> 1.19 us
  other arithmetic: 1.42 us -> 0 us
    pallas_call x1, Pallas kernels: 126 us -> 118 us  [body(): pl.pallas_call(kernel, out_shape=jax.ShapeDtypeStruct((8, 128), F32), in_...]
    unnamed x12 -> x0, local copies, waits for them, and re-layouts: 6.18 us -> none
where the time goes in v1:
time: 120 us
  Pallas kernels  118 us (98%)
    pallas_call x1, Pallas kernels, body(): pl.pallas_call(kernel, out_shape=jax.ShapeDtypeStruct((8, 128), F32), in_...  118 us

profile of v1, /device:TPU:1, one launch (start us, length us, event | category | flops | bytes accessed | tf_op | source)
XLA Modules:
  0.0 119.5 jit_solution(1059328770045809428)
XLA Ops:
  0.7 117.7 %shard_map.91 = f32[8,128]{1,0:T(8,128)} custom-call(s32[1]{0:T(128)S(6)} %copy.10.span_ref, bf16[8,8192]{1,0:T(8,128)(2,1)} %q_ref.1, bf16[64,1024]{1,0:T(8,128)(2,1)} %k_ref.1, bf16[64,1024]{1,0:T(8,128)(2,1)} %v_ref.1, bf16[128,640]{1,0:T(8,128)(2,1)} %w_ref.1, bf16[8,640]{1,0:T(8,128)(2,1)} %res_ref.1, bf16[5120]{0:T(1024)(128)(2,1)} %gain_ref.1, ...), custom_call_target="tpu_custom_call" | custom-call | flops 3000000000 | bytes 8000000 | tf_op jit(solution)/shard_map/pallas_call | solution.py:673
  118.3 1.2 slice_bitcast_fusion

commit v2 on v1

--- a/solution.py
+++ b/solution.py
@@ -74,6 +74,8 @@
     hsend,
     hall,
     whead,
+    hid_m,
+    sq_m,
     logit,
     stsrc,
     stz,
@@ -106,6 +108,8 @@
     h1_r,
     h2_s,
     h2_r,
+    h3_s,
+    h3_r,
     hw_s,
     hw_r,
     t1_s,
@@ -118,21 +122,21 @@
     v = lax.axis_index("vocab")
     z, y, x, c = s // NY, s % NY, v // NC, v % NC
     g, par = z // 2, z % 2
+    half = z // 8
+    z_low = z - 8 * half
     q = y * NX + x
 
     def dev(zz, yy, xx, cc):
         return (zz * NY + yy, xx * NC + cc)
 
     def wrap(a, n):
-        return lax.rem(a + n, n)
-
-    def flip(a, k):
-        swaps = (a, a + 1 - 2 * lax.rem(a, 2), lax.rem(a + 2, 4), 3 - a)
-        if isinstance(k, int):
-            return swaps[k]
-        return jnp.where(
-            k < 2, jnp.where(k == 0, swaps[0], swaps[1]), jnp.where(k == 2, swaps[2], swaps[3])
-        )
+        return jnp.where(a >= n, a - n, a)
+
+    def flips(a):
+        odd = a % 2
+        return (a, a + 1 - 2 * odd, wrap(a + 2, 4), 3 - a)
+
+    flip_x, flip_y = flips(x), flips(y)
 
     def push(src, dst, ss, rs, to):
         cp = pltpu.make_async_remote_copy(
@@ -183,7 +187,7 @@
     greet(z, y, x, 1 - c)
     for k in range(1, 16):
         for cc in range(NC):
-            greet(z, flip(y, k // 4), flip(x, k % 4), cc)
+            greet(z, flip_y[k // 4], flip_x[k % 4], cc)
 
     for cp in loads:
         cp.wait()
@@ -215,7 +219,6 @@
             push(src.at[:, cols], dst.at[y, k], kv_s.at[d, i], kv_r.at[k, i], to)
 
     spread(k_ref, kbuf, 0)
-    spread(v_ref, vbuf, 1)
 
     for d in range(1, NY):
         push(w_ref, wbuf.at[par, y], w_s.at[d], w_r.at[par, y], dev(z, wrap(y + d, NY), x, c))
@@ -230,8 +233,8 @@
     tgt4 = tgt_m[...].reshape(4, 128).astype(F32)
     src = lax.broadcasted_iota(jnp.int32, (128, 256), 0)
     dst = lax.broadcasted_iota(jnp.int32, (128, 256), 1)
-    plane_of = lax.rem(dst // 32 + z, 8)
-    here = src == (plane_of % 4) * 32 + dst % 32
+    plane_of = lax.rem((dst // 8) % 8 + z, 8)
+    here = src == (plane_of % 4) * 32 + (dst // 64) * 8 + dst % 8
     ordered = jnp.zeros((8, 256), F32)
     for r in range(2):
         row = jnp.where(c == 0, tgt4[r : r + 1], tgt4[2 + r : 3 + r])
@@ -265,10 +268,16 @@
         (ci == from_row).astype(BF16), q_rows, preferred_element_type=F32
     ).astype(BF16)
 
+    @pl.loop(1, 8)
+    def _(d):
+        got(kbuf.at[0, 0], kv_s.at[d, 0])
+
+    spread(v_ref, vbuf, 1)
+
     @pl.loop(1, NV)
     def _(k):
         o = wrap(v + k, NV)
-        push(qall.at[v], qall.at[v], qa_s.at[k], qa_r.at[v], dev(z, y, o // NC, o % NC))
+        push(qall.at[v], qall.at[v], qa_s.at[k], qa_r.at[v], (s, o))
 
     def forward(buf, i, ss, rs):
         @pl.loop(0, 8)
@@ -334,7 +343,7 @@
 
                 @pl.when(v != o)
                 def _():
-                    push(osend.at[o], obuf.at[v], o_s.at[o], o_r.at[v], dev(z, y, o // NC, o % NC))
+                    push(osend.at[o], obuf.at[v], o_s.at[o], o_r.at[v], (s, o))
 
     def arrived(e, buf, rs):
         yy = wrap(y - e + NY, NY)
@@ -405,7 +414,7 @@
     @pl.loop(1, NV)
     def _(k):
         o = wrap(v + k, NV)
-        push(mine, abuf.at[v], a_s.at[k], a_r.at[v], dev(z, y, o // NC, o % NC))
+        push(mine, abuf.at[v], a_s.at[k], a_r.at[v], (s, o))
 
     abuf[v] = att[pl.ds(pl.multiple_of(par * 64, 64), 64), :]
     for d in range(1, NY):
@@ -441,89 +450,105 @@
         hidden = hidden + prbuf[frm].astype(F32)
     hsend[...] = (hidden * gain_n[v]).astype(BF16)
 
-    half = z // 8
-
     @pl.loop(1, NZ)
     def _(d):
         to = wrap(z + d, NZ)
-        k = lax.rem(z + 16 - to, 8)
-        push(hsend, hall.at[x, k, y, c], h_s.at[d], h_r.at[k, c], dev(to, y, x, half))
+        k = wrap(wrap(z_low - to + 16, 16), 8)
+        slot = hall.at[k // 4, x, y, k % 4, c]
+        push(hsend, slot, h_s.at[d], h_r.at[k, c], dev(to, y, x, half))
 
     @pl.when(c == half)
     def _():
-        keep = pltpu.make_async_copy(hsend, hall.at[x, 0, y, c], h_r.at[0, c])
+        keep = pltpu.make_async_copy(hsend, hall.at[0, x, y, 0, c], h_r.at[0, c])
         keep.start()
 
     @pl.when(c != half)
     def _():
-        push(hsend, hall.at[x, 0, y, c], h_s.at[0], h_r.at[0, c], dev(z, y, x, half))
-
-    def block(xx, yy, i):
-        return hall.at[xx, pl.ds(2 * i, 2), yy]
-
-    def first_step(i, x_first):
-        for k in (2 * i, 2 * i + 1):
+        push(hsend, hall.at[0, x, y, 0, c], h_s.at[0], h_r.at[0, c], dev(z, y, x, half))
+
+    def piece(i, a, b):
+        xx, yy = (a, b) if i == 0 else (b, a)
+        return hall.at[i, xx, yy]
+
+    def first_dev(i, d):
+        return dev(z, y, wrap(x + d, NX), c) if i == 0 else dev(z, wrap(y + d, NY), x, c)
+
+    def second_dev(i, d):
+        return dev(z, wrap(y + d, NY), x, c) if i == 0 else dev(z, y, wrap(x + d, NX), c)
+
+    def settle(i, xx, yy):
+        rows = pl.ds(pl.multiple_of(yy * 64 + i * 32, 32), 32)
+        squares = jnp.zeros((32, 128), F32)
+        for cc in range(NC):
+            hid = hall[i, xx, yy, :, cc].astype(F32).reshape(32, COLS)
+            n = xx * NC + cc
+            inv = ginv_n[n]
+            for t in range(COLS // 128):
+                part = hid[:, t * 128 : (t + 1) * 128]
+                squares = squares + part * part * inv[0:1, t * 128 : (t + 1) * 128]
+            cols = pl.ds(pl.multiple_of(n * COLS, 128), COLS)
+            hid_m[rows, cols] = hid.astype(BF16)
+        sq_m[rows, :] += squares
+
+    def settle_line(i, b):
+        @pl.loop(0, 4)
+        def _(a):
+            if i == 0:
+                settle(i, a, b)
+            else:
+                settle(i, b, a)
+
+    sq_m[...] = jnp.zeros_like(sq_m)
+    lead, cross = (x, y), (y, x)
+    for i in range(2):
+        for k in range(4 * i, 4 * i + 4):
             for cc in range(NC):
-                got(hall.at[x, k, y, cc], h_r.at[k, cc])
+                got(hall.at[k // 4, x, y, k % 4, cc], h_r.at[k, cc])
         for d in (1, 3, 2):
-            to = dev(z, y, wrap(x + d, NX), c) if x_first else dev(z, wrap(y + d, NY), x, c)
-            here = x if x_first else y
-            push(block(x, y, i), block(x, y, i), h1_s.at[i, d], h1_r.at[i, here], to)
-
-    def second_step(i, x_first):
-        for e in (0, 1, 3, 2):
-            xx = wrap(x + e, NX) if x_first else x
-            yy = y if x_first else wrap(y + e, NY)
-            there, here = (xx, y) if x_first else (yy, x)
-            if e > 0:
-                got(block(xx, yy, i), h1_r.at[i, there])
-            for d in (1, 3, 2):
-                to = dev(z, wrap(y + d, NY), x, c) if x_first else dev(z, y, wrap(x + d, NX), c)
-                push(
-                    block(xx, yy, i),
-                    block(xx, yy, i),
-                    h2_s.at[i, e, d],
-                    h2_r.at[i, here, there],
-                    to,
-                )
-
-    def arrivals(i, x_first):
-        for d in range(1, 4):
-            for e in range(4):
-                frm = wrap((y if x_first else x) + d, 4)
-                xx, yy = (e, frm) if x_first else (frm, e)
-                got(block(xx, yy, i), h2_r.at[i, frm, e])
-
-    first_step(0, True)
-    first_step(3, False)
-    second_step(0, True)
-    first_step(1, True)
-    second_step(3, False)
-    first_step(2, False)
-    second_step(1, True)
-    second_step(2, False)
-
+            own = piece(i, lead[i], cross[i])
+            push(own, own, h1_s.at[i, d], h1_r.at[i, lead[i]], first_dev(i, d))
+
+    def send_second(i, a, up):
+        own = piece(i, a, cross[i])
+        push(own, own, h2_s.at[i, a, up], h2_r.at[i, a, up], second_dev(i, 1 if up else 3))
+
+    for a, up in ((0, 0), (2, 1), (1, 0), (3, 1)):
+        for i in range(2):
+
+            @pl.when(lead[i] != a)
+            def _():
+                got(piece(i, a, cross[i]), h1_r.at[i, a])
+
+            send_second(i, a, up)
+    for a, up in ((0, 1), (2, 0), (1, 1), (3, 0)):
+        for i in range(2):
+            send_second(i, a, up)
+
+    for a, up in ((0, 0), (2, 1), (1, 0), (3, 1)):
+        for i in range(2):
+            frm = wrap(cross[i] + (3 if up else 1), 4)
+            there = piece(i, a, frm)
+            got(there, h2_r.at[i, a, up])
+            push(there, there, h3_s.at[i, a], h3_r.at[i, a], second_dev(i, 1 if up else 3))
+
+    for i in range(2):
+        settle_line(i, cross[i])
+    for i in range(2):
+        for a, up in ((0, 1), (2, 0), (1, 1), (3, 0)):
+            got(piece(i, a, wrap(cross[i] + (3 if up else 1), 4)), h2_r.at[i, a, up])
+        settle_line(i, wrap(cross[i] + 1, 4))
+        settle_line(i, wrap(cross[i] + 3, 4))
     own_head.wait()
     got(whead.at[1], hw_r.at[0])
-    for i, x_first in ((0, True), (3, False), (1, True), (2, False)):
-        arrivals(i, x_first)
-
-    logit[...] = jnp.zeros_like(logit)
-
-    def head_step(n, squares):
-        hid = hall[n // 2, :, :, lax.rem(n, 2)].astype(F32).reshape(256, COLS)
-        inv = ginv_n[n]
-        for t in range(COLS // 128):
-            part = hid[:, t * 128 : (t + 1) * 128]
-            squares = squares + part * part * inv[0:1, t * 128 : (t + 1) * 128]
-        hid16 = hid.astype(BF16)
-        cols = pl.ds(pl.multiple_of(n * COLS, 128), COLS)
-        for p in range(2):
-            logit[p] += nt(whead[p, :, cols], hid16)
-        return squares
-
-    squares = lax.fori_loop(0, NV, head_step, jnp.zeros((256, 128), F32))
-    sums = nt(jnp.ones((8, 128), F32), squares, lax.Precision.HIGHEST)
+    for i in range(2):
+        for a in range(4):
+            got(piece(i, a, wrap(cross[i] + 2, 4)), h3_r.at[i, a])
+        settle_line(i, wrap(cross[i] + 2, 4))
+
+    for p in range(2):
+        logit[p] = nt(whead[p], hid_m[...])
+
+    sums = nt(jnp.ones((8, 128), F32), sq_m[...], lax.Precision.HIGHEST)
     row_scale = lax.rsqrt(sums[0:1] / WIDTH + FLOOR)
     targets = tgt_n[0:1]
     row_id = lax.broadcasted_iota(jnp.int32, (ROWS, 256), 0)
@@ -544,7 +569,9 @@
     )
     stsrc[...] = jnp.zeros_like(stsrc)
     for k in range(8):
-        stsrc[k, :, 0:32] = stats[:, k * 32 : (k + 1) * 32]
+        for yy in range(NY):
+            first = yy * 64 + k * 8
+            stsrc[k, :, yy * 8 : (yy + 1) * 8] = stats[:, first : first + 8]
 
     def join_all(ref, n):
         m = ref[0, 0:1]
@@ -559,7 +586,7 @@
 
     @pl.loop(0, 8)
     def _(k):
-        to = 8 * c + lax.rem(z + k, 8)
+        to = 8 * c + wrap(z_low + k, 8)
 
         @pl.when(to != z)
         def _():
@@ -580,7 +607,7 @@
         push(stred, stfin.at[q], t2_s.at[0, 0], t2_r.at[q], dev(z, y, x, 1 - c))
         for k in (1, 4, 3, 12, 2, 8, 5, 15, 6, 9, 7, 13, 10, 11, 14):
             for cc in range(NC):
-                to = dev(z, flip(y, k // 4), flip(x, k % 4), cc)
+                to = dev(z, flip_y[k // 4], flip_x[k % 4], cc)
                 push(stred, stfin.at[q], t2_s.at[k, cc], t2_r.at[q], to)
         stfin[q] = stred[...]
 
@@ -589,7 +616,7 @@
         got(stfin.at[q], t2_r.at[q])
 
     for k in range(1, 16):
-        o = flip(y, k // 4) * NX + flip(x, k % 4)
+        o = flip_y[k // 4] * NX + flip_x[k % 4]
         got(stfin.at[o], t2_r.at[o])
 
     m, t, picked = join_all(stfin, 16)
@@ -608,7 +635,6 @@
 
     @pl.loop(1, 8)
     def _(d):
-        got(kbuf.at[0, 0], kv_s.at[d, 0])
         got(vbuf.at[0, 0], kv_s.at[d, 1])
         got(qall.at[0], qa_s.at[d])
         got(prsend.at[0], pr_s.at[d])
@@ -633,16 +659,17 @@
     got(whead.at[1], hw_s.at[0])
     got(psrc, p_s.at[0])
 
-    @pl.loop(0, 4)
-    def _(i):
+    for i in range(2):
         for d in range(1, 4):
-            got(hall.at[0, pl.ds(0, 2), 0], h1_s.at[i, d])
-            for e in range(4):
-                got(hall.at[0, pl.ds(0, 2), 0], h2_s.at[i, e, d])
+            got(piece(i, 0, 0), h1_s.at[i, d])
+        for a in range(4):
+            got(piece(i, 0, 0), h2_s.at[i, a, 0])
+            got(piece(i, 0, 0), h2_s.at[i, a, 1])
+            got(piece(i, 0, 0), h3_s.at[i, a])
 
     @pl.loop(0, 8)
     def _(k):
-        @pl.when(8 * c + lax.rem(z + k, 8) != z)
+        @pl.when(8 * c + wrap(z_low + k, 8) != z)
         def _():
             got(stsrc.at[0], t1_s.at[k])
 
@@ -703,8 +730,10 @@
             pltpu.VMEM((8, 8, COLS), BF16),
             pltpu.VMEM((8, 8, COLS), BF16),
             pltpu.VMEM((8, COLS), BF16),
-            pltpu.VMEM((NX, 8, NY, NC, 8, COLS), BF16),
+            pltpu.VMEM((2, NX, NY, 4, NC, 8, COLS), BF16),
             pltpu.VMEM((2, ROWS, WIDTH), BF16),
+            pltpu.VMEM((256, WIDTH), BF16),
+            pltpu.VMEM((256, 128), F32),
             pltpu.VMEM((2, ROWS, 256), F32),
             pltpu.VMEM((8, 8, 128), F32),
             pltpu.VMEM((NZ, 8, 128), F32),
@@ -733,10 +762,12 @@
             dma((8,)),
             dma((NZ,)),
             dma((8, NC)),
-            dma((4, 4)),
-            dma((4, 4)),
-            dma((4, 4, 4)),
-            dma((4, 4, 4)),
+            dma((2, 4)),
+            dma((2, 4)),
+            dma((2, 4, 2)),
+            dma((2, 4, 2)),
+            dma((2, 4)),
+            dma((2, 4)),
             dma((1,)),
             dma((1,)),
             dma((8,)),

time: 120 us -> 113 us (0.942)
  Pallas kernels: 118 us -> 111 us
    pallas_call x1, Pallas kernels: 118 us -> 111 us  [body(): pl.pallas_call(kernel, out_shape=jax.ShapeDtypeStruct((8, 128), F32), in_...]
where the time goes in v2:
time: 113 us
  Pallas kernels  111 us (98%)
  local copies, waits for them, and re-layouts  1.19 us (1%)
    pallas_call x1, Pallas kernels, body(): pl.pallas_call(kernel, out_shape=jax.ShapeDtypeStruct((8, 128), F32), in_...  111 us

profile of v2, /device:TPU:1, one launch (start us, length us, event | category | flops | bytes accessed | tf_op | source)
XLA Modules:
  0.0 113.2 jit_solution(15926439133936314211)
XLA Ops:
  0.7 111.4 %shard_map.91 = f32[8,128]{1,0:T(8,128)} custom-call(s32[1]{0:T(128)S(6)} %copy.10.span_ref, bf16[8,8192]{1,0:T(8,128)(2,1)} %q_ref.1, bf16[64,1024]{1,0:T(8,128)(2,1)} %k_ref.1, bf16[64,1024]{1,0:T(8,128)(2,1)} %v_ref.1, bf16[128,640]{1,0:T(8,128)(2,1)} %w_ref.1, bf16[8,640]{1,0:T(8,128)(2,1)} %res_ref.1, bf16[5120]{0:T(1024)(128)(2,1)} %gain_ref.1, ...), custom_call_target="tpu_custom_call" | custom-call | flops 3000000000 | bytes 8000000 | tf_op jit(solution)/shard_map/pallas_call | solution.py:700
  112.0 1.2 %slice_bitcast_fusion = f32[8]{0:T(128)} fusion(f32[8,128]{1,0:T(8,128)} %shard_map.91), kind=kLoop, calls=%fused_computation | loop fusion | bytes 64 | tf_op jit(solution)/shard_map/squeeze | solution.py:796

commit v3 on v2

--- a/solution.py
+++ b/solution.py
@@ -428,10 +428,10 @@
         got(abuf.at[frm], a_r.at[frm])
 
     rows_f = abuf[...].astype(F32)
-    proj = jnp.zeros((64, COLS), F32)
-    for h in range(8):
-        rows = rows_f[:, h * 8 : (h + 1) * 8, :].reshape(64, 128).astype(BF16)
-        proj = proj + jnp.dot(rows, wbuf[h // 4, h % 4], preferred_element_type=F32)
+    rows = jnp.concatenate(
+        [rows_f[:, h * 8 : (h + 1) * 8, :].reshape(64, 128) for h in range(8)], axis=1
+    ).astype(BF16)
+    proj = jnp.dot(rows, wbuf[...].reshape(1024, COLS), preferred_element_type=F32)
     r64 = lax.broadcasted_iota(jnp.int32, (64, 64), 0)
     c64 = lax.broadcasted_iota(jnp.int32, (64, 64), 1)
     to_planes = (c64 == (r64 % 8) * 8 + r64 // 8).astype(BF16)
@@ -508,41 +508,37 @@
             own = piece(i, lead[i], cross[i])
             push(own, own, h1_s.at[i, d], h1_r.at[i, lead[i]], first_dev(i, d))
 
-    def send_second(i, a, up):
-        own = piece(i, a, cross[i])
-        push(own, own, h2_s.at[i, a, up], h2_r.at[i, a, up], second_dev(i, 1 if up else 3))
-
-    for a, up in ((0, 0), (2, 1), (1, 0), (3, 1)):
+    def send_second(i, e, up):
+        own = piece(i, wrap(lead[i] + e, 4), cross[i])
+        push(own, own, h2_s.at[i, e, up], h2_r.at[i, e, up], second_dev(i, 1 if up else 3))
+
+    for e, up in ((0, 1), (0, 0), (1, 0), (3, 1), (1, 1), (3, 0), (2, 0), (2, 1)):
         for i in range(2):
-
-            @pl.when(lead[i] != a)
-            def _():
+            if (e, up) in ((1, 0), (3, 1), (2, 0)):
+                a = wrap(lead[i] + e, 4)
                 got(piece(i, a, cross[i]), h1_r.at[i, a])
-
-            send_second(i, a, up)
-    for a, up in ((0, 1), (2, 0), (1, 1), (3, 0)):
+            send_second(i, e, up)
+
+    onward = ((0, 1), (1, 0), (3, 1), (2, 0))
+    for e, up in onward:
         for i in range(2):
-            send_second(i, a, up)
-
-    for a, up in ((0, 0), (2, 1), (1, 0), (3, 1)):
-        for i in range(2):
-            frm = wrap(cross[i] + (3 if up else 1), 4)
-            there = piece(i, a, frm)
-            got(there, h2_r.at[i, a, up])
-            push(there, there, h3_s.at[i, a], h3_r.at[i, a], second_dev(i, 1 if up else 3))
+            there = piece(i, wrap(lead[i] + e, 4), wrap(cross[i] + (3 if up else 1), 4))
+            got(there, h2_r.at[i, e, up])
+            push(there, there, h3_s.at[i, e], h3_r.at[i, e], second_dev(i, 1 if up else 3))
 
     for i in range(2):
         settle_line(i, cross[i])
     for i in range(2):
-        for a, up in ((0, 1), (2, 0), (1, 1), (3, 0)):
-            got(piece(i, a, wrap(cross[i] + (3 if up else 1), 4)), h2_r.at[i, a, up])
+        for e, up in onward:
+            there = piece(i, wrap(lead[i] + e, 4), wrap(cross[i] + (1 if up else 3), 4))
+            got(there, h2_r.at[i, e, 1 - up])
         settle_line(i, wrap(cross[i] + 1, 4))
         settle_line(i, wrap(cross[i] + 3, 4))
     own_head.wait()
     got(whead.at[1], hw_r.at[0])
     for i in range(2):
-        for a in range(4):
-            got(piece(i, a, wrap(cross[i] + 2, 4)), h3_r.at[i, a])
+        for e in range(4):
+            got(piece(i, wrap(lead[i] + e, 4), wrap(cross[i] + 2, 4)), h3_r.at[i, e])
         settle_line(i, wrap(cross[i] + 2, 4))
 
     for p in range(2):

time: 113 us -> 112 us (level)
    pallas_call x1, Pallas kernels: 111 us -> 110 us  [body(): pl.pallas_call(kernel, out_shape=jax.ShapeDtypeStruct((8, 128), F32), in_...]
where the time goes in v3:
time: 112 us
  Pallas kernels  110 us (98%)
  local copies, waits for them, and re-layouts  1.19 us (1%)
    pallas_call x1, Pallas kernels, body(): pl.pallas_call(kernel, out_shape=jax.ShapeDtypeStruct((8, 128), F32), in_...  110 us

profile of v3, /device:TPU:1, one launch (start us, length us, event | category | flops | bytes accessed | tf_op | source)
XLA Modules:
  0.0 111.6 jit_solution(12339503153409895270)
XLA Ops:
  0.7 109.8 %shard_map.91 = f32[8,128]{1,0:T(8,128)} custom-call(s32[1]{0:T(128)S(6)} %copy.10.span_ref, bf16[8,8192]{1,0:T(8,128)(2,1)} %q_ref.1, bf16[64,1024]{1,0:T(8,128)(2,1)} %k_ref.1, bf16[64,1024]{1,0:T(8,128)(2,1)} %v_ref.1, bf16[128,640]{1,0:T(8,128)(2,1)} %w_ref.1, bf16[8,640]{1,0:T(8,128)(2,1)} %res_ref.1, bf16[5120]{0:T(1024)(128)(2,1)} %gain_ref.1, ...), custom_call_target="tpu_custom_call" | custom-call | flops 3000000000 | bytes 8000000 | tf_op jit(solution)/shard_map/pallas_call | solution.py:696
  110.4 1.2 %slice_bitcast_fusion = f32[8]{0:T(128)} fusion(f32[8,128]{1,0:T(8,128)} %shard_map.91), kind=kLoop, calls=%fused_computation | loop fusion | bytes 64 | tf_op jit(solution)/shard_map/squeeze | solution.py:792

commit v4 on v3

--- a/solution.py
+++ b/solution.py
@@ -202,11 +202,6 @@
 
     pl.semaphore_wait(barrier, 2 * (NZ - 1) + 31)
 
-    @pl.loop(1, NZ)
-    def _(d):
-        to = wrap(z + d, NZ)
-        push(q1src.at[to // 2], q1buf.at[z], q1_s.at[d], q1_r.at[z], dev(to, y, x, c))
-
     def spread(src, dst, i):
         @pl.loop(1, 8)
         def _(d):
@@ -219,6 +214,11 @@
             push(src.at[:, cols], dst.at[y, k], kv_s.at[d, i], kv_r.at[k, i], to)
 
     spread(k_ref, kbuf, 0)
+
+    @pl.loop(1, NZ)
+    def _(d):
+        to = wrap(z + d, NZ)
+        push(q1src.at[to // 2], q1buf.at[z], q1_s.at[d], q1_r.at[z], dev(to, y, x, c))
 
     for d in range(1, NY):
         push(w_ref, wbuf.at[par, y], w_s.at[d], w_r.at[par, y], dev(z, wrap(y + d, NY), x, c))
@@ -439,7 +439,8 @@
     prsend[...] = by_plane.reshape(8, 8, COLS).astype(BF16)
 
     @pl.loop(1, 8)
-    def _(d):
+    def _(i):
+        d = jnp.where(i % 2 == 1, (i + 1) // 2, 8 - i // 2)
         to = wrap(g + d, 8)
         push(prsend.at[to], prbuf.at[g], pr_s.at[d], pr_r.at[g], dev(2 * to + par, y, x, c))
 
@@ -451,7 +452,8 @@
     hsend[...] = (hidden * gain_n[v]).astype(BF16)
 
     @pl.loop(1, NZ)
-    def _(d):
+    def _(i):
+        d = jnp.where(i % 2 == 1, (i + 1) // 2, NZ - i // 2)
         to = wrap(z + d, NZ)
         k = wrap(wrap(z_low - to + 16, 16), 8)
         slot = hall.at[k // 4, x, y, k % 4, c]

time: 112 us -> 116 us (1.036)
  Pallas kernels: 110 us -> 114 us
    pallas_call x1, Pallas kernels: 110 us -> 114 us  [body(): pl.pallas_call(kernel, out_shape=jax.ShapeDtypeStruct((8, 128), F32), in_...]
where the time goes in v4:
time: 116 us
  Pallas kernels  114 us (98%)
  local copies, waits for them, and re-layouts  1.19 us (1%)
    pallas_call x1, Pallas kernels, body(): pl.pallas_call(kernel, out_shape=jax.ShapeDtypeStruct((8, 128), F32), in_...  114 us

profile of v4, /device:TPU:1, one launch (start us, length us, event | category | flops | bytes accessed | tf_op | source)
XLA Modules:
  0.0 115.7 jit_solution(4092785933346671696)
XLA Ops:
  0.7 113.9 %shard_map.91 = f32[8,128]{1,0:T(8,128)} custom-call(s32[1]{0:T(128)S(6)} %copy.10.span_ref, bf16[8,8192]{1,0:T(8,128)(2,1)} %q_ref.1, bf16[64,1024]{1,0:T(8,128)(2,1)} %k_ref.1, bf16[64,1024]{1,0:T(8,128)(2,1)} %v_ref.1, bf16[128,640]{1,0:T(8,128)(2,1)} %w_ref.1, bf16[8,640]{1,0:T(8,128)(2,1)} %res_ref.1, bf16[5120]{0:T(1024)(128)(2,1)} %gain_ref.1, ...), custom_call_target="tpu_custom_call" | custom-call | flops 3000000000 | bytes 8000000 | tf_op jit(solution)/shard_map/pallas_call | solution.py:698
  114.5 1.2 %slice_bitcast_fusion = f32[8]{0:T(128)} fusion(f32[8,128]{1,0:T(8,128)} %shard_map.91), kind=kLoop, calls=%fused_computation | loop fusion | bytes 64 | tf_op jit(solution)/shard_map/squeeze | solution.py:794
